TPU v7x, 512 devices: a whole 4x8x8 slice. The times are simulated.
512 devices in a mesh: pb: 32 (over z_hi, y, core), dev: 16 (over x, z_lo).
Axes of the slice: x: 4, y: 8, z: 8 (z_hi: 2, z_lo: 4; z = z_hi * 4 + z_lo), core: 2. Of those that a mesh axis runs over, the one named last changes fastest.
Arguments:
- query_factors: float32 [32768, 128], P('pb'), may hold values from -2.4 to 2.4
- panel_factors: float32 [131072, 128], P(('pb', 'dev')), may hold values from -2.4 to 2.4
- query_weight: float32 [32768], P('pb'), may hold values from 1 to 144, as said below
- plan: int32 [32], replicated, may hold values from 0 to 31, each once
- tile_seeds: int32 [32, 32], replicated, may hold values from 0 to 65520
Outputs:
- query_out: float32 [32768, 128], P('pb')
- panel_out: float32 [131072, 128], P(('pb', 'dev'))
Inputs may be any that keep to these rules, and one draw needn't show every extreme that they name: `query_weight`: each row's weight is positive and at most 144.
All inputs are finite; a program needn't handle non-finite values.
Results may differ from a plain program's by a relative error of at most 0.00018.
Values sent between devices are 32-bit elements; how exact they have to be, the bound alone decides.
A program may use at most 64 MiB of HBM per device.

v0:
```python
import jax
import jax.numpy as jnp
from jax import lax
from jax.sharding import Mesh
from jax.sharding import PartitionSpec as P

STRATA = 3
PB = ("pb_0", "pb_1", "pb_2")
DEV = ("dev_0", "dev_1")
PB_DEV = ("pb_0", "pb_1", "pb_2", "dev_0", "dev_1")
epsilon = 1e-06
learning_rate = 0.3


def in_blocks(array, dim, size):
    before, after = (array.shape[:dim], array.shape[dim + 1 :])
    return jnp.moveaxis(array.reshape(*before, size, -1, *after), dim, 0)


def sent_and_summed(array, axis, dim):
    size = lax.axis_size(axis)
    parts = lax.all_to_all(in_blocks(array, dim, size), axis, 0, 0, tiled=True)
    return jnp.sum(parts, axis=0)


def one_axis_at_a_time(array, axes):
    for axis in axes:
        array = lax.psum(array, axis)
    return array


def sent_to_all(array, axis):
    copies = jnp.broadcast_to(array, (lax.axis_size(axis), *array.shape))
    return lax.all_to_all(copies, axis, split_axis=0, concat_axis=0, tiled=True)


def laid_out(parts, dim):
    parts = jnp.moveaxis(parts, 0, dim)
    shape = parts.shape
    return parts.reshape(*shape[:dim], shape[dim] * shape[dim + 1], *shape[dim + 2 :])


def gather_directly(array, axis, dim):
    parts = sent_to_all(array, axis)
    return laid_out(parts, dim)


def shifted(array, axis, by):
    size = lax.axis_size(axis)
    return lax.ppermute(array, axis, [(i, (i + by) % size) for i in range(size)])


def shift_down(mixed, count):
    return lax.shift_right_logical(mixed, jnp.full(mixed.shape, count, jnp.int32))


def hashed(tile_seed, row_ids, col_ids):
    mixed = tile_seed * 374761393 + row_ids * 668265263 + col_ids * 1274126177
    mixed = mixed ^ shift_down(mixed, 15)
    mixed = mixed * 73244475
    mixed = mixed ^ shift_down(mixed, 13)
    mixed = mixed * 1911520717
    mixed = mixed ^ shift_down(mixed, 16)
    return (mixed & 65535).astype(jnp.float32) / 32768.0 - 1.0


def per_device(query_factors, panel_factors, query_weight, plan, tile_seeds):
    groups = lax.axis_size(PB)
    spread = lax.axis_size(DEV)
    position = lax.axis_index(PB)
    column = lax.axis_index(DEV)
    rows_here = query_factors.shape[0]
    cols_here = panel_factors.shape[0]
    factor_rank = query_factors.shape[1]
    u_count = float(rows_here * groups * factor_rank)
    v_count = float(cols_here * groups * spread * factor_rank)
    row_ids = position * rows_here + jnp.arange(rows_here, dtype=jnp.int32)[:, None]
    local_cols = jnp.arange(cols_here, dtype=jnp.int32)[None, :]
    factors = query_factors
    panel = panel_factors
    for stratum in range(STRATA):
        panel_id = plan[jnp.mod(position - stratum, groups)]
        tile_seed = tile_seeds[position, panel_id]
        col_ids = (panel_id * spread + column) * cols_here + local_cols
        scores = hashed(tile_seed, row_ids, col_ids)
        approx = jnp.dot(factors, panel.T, precision=lax.Precision.HIGHEST)
        weighted = query_weight[:, None] * (scores - approx)
        part_u = jnp.dot(weighted, panel, precision=lax.Precision.HIGHEST)
        grad_v = jnp.dot(weighted.T, factors, precision=lax.Precision.HIGHEST)
        norm_v = jnp.sum(grad_v * grad_v)
        share = sent_and_summed(part_u, DEV, 0)
        totals = (
            one_axis_at_a_time(jnp.sum(share * share), PB_DEV),
            one_axis_at_a_time(norm_v, PB_DEV),
        )
        step_u = learning_rate / jnp.sqrt(totals[0] / u_count + epsilon)
        share_rows = share.shape[0]
        own_rows = lax.dynamic_slice_in_dim(factors, column * share_rows, share_rows, 0)
        factors = gather_directly(own_rows + step_u * share, DEV, 0)
        step_v = learning_rate / jnp.sqrt(totals[1] / v_count + epsilon)
        panel = shifted(panel + step_v * grad_v, PB, 1)
    return (factors, panel)


def solution(mesh):
    finer = Mesh(mesh.devices.reshape(2, 8, 2, 4, 4), ("pb_0", "pb_1", "pb_2", "dev_0", "dev_1"))
    return jax.shard_map(
        per_device,
        mesh=finer,
        in_specs=(P(PB, None), P(PB_DEV, None), P(PB), P(), P()),
        out_specs=(P(PB, None), P(PB_DEV, None)),
        check_vma=False,
    )
```

profile of v0, /device:TPU:2, one launch (start us, length us, event | category | flops | bytes accessed | tf_op | source)
XLA Modules:
  0.0 296.0 jit_solution(11714593561061236251)
XLA Ops:
  0.7 1.4 fusion.25
  8.6 1.5 fusion.24
  10.7 2.3 fusion.2
  13.1 1.8 fusion.26
  14.9 10.4 %all-to-all-start = ((f32[16,64,128]{2,1,0:T(8,128)}), f32[16,64,128]{2,1,0:T(8,128)S(1)}, u32[]{:S(2)}, u32[]{:S(2)}) async-start(f32[16,64,128]{2,1,0:T(8,128)} %bitcast.2), calls=%async_computation | async-start | bytes 1048576 | tf_op jit(solution)/shard_map/all_to_all | solution.py:22
  25.3 2.4 multiply_reduce_fusion.2
  27.7 11.5 %all-to-all-done = f32[16,64,128]{2,1,0:T(8,128)S(1)} async-done(((f32[16,64,128]{2,1,0:T(8,128)}), f32[16,64,128]{2,1,0:T(8,128)S(1)}, u32[]{:S(2)}, u32[]{:S(2)}) %all-to-all-start) | async-done | bytes 524320 | tf_op jit(solution)/shard_map/all_to_all | solution.py:22
  39.2 0.6 multiply_reduce_fusion.5
  39.8 9.9 %all-reduce.14 = (f32[]{:T(128)}, f32[]{:T(128)}) all-reduce(f32[]{:T(128)} %multiply_reduce_fusion.5, f32[]{:T(128)} %get-tuple-element.38), channel_id=1, replica_groups=mesh['pb_0'=2,'pb_1'=8,'pb_2'=2,'dev_0'=4,'dev_1'=4] {'pb_0'}, use_global_device_ids=true, to_apply=%region_2.3 | all-reduce | flops 2 | bytes 16 | tf_op jit(solution)/shard_map/psum | solution.py:28
  49.7 18.3 %all-reduce.2 = (f32[]{:T(128)}, f32[]{:T(128)}) all-reduce(f32[]{:T(128)} %get-tuple-element.30, f32[]{:T(128)} %get-tuple-element.31), channel_id=1, replica_groups=mesh['pb_0'=2,'pb_1'=8,'pb_2'=2,'dev_0'=4,'dev_1'=4] {'pb_1'}, use_global_device_ids=true, to_apply=%region_3.4 | all-reduce | flops 2 | bytes 16 | tf_op jit(solution)/shard_map/psum | solution.py:28
  68.0 3.1 %all-reduce.11 = (f32[]{:T(128)}, f32[]{:T(128)}) all-reduce(f32[]{:T(128)} %get-tuple-element.6, f32[]{:T(128)} %get-tuple-element.7), channel_id=1, replica_groups=mesh['pb_0'=2,'pb_1'=8,'pb_2'=2,'dev_0'=4,'dev_1'=4] {'pb_2'}, use_global_device_ids=true, to_apply=%region_4.5 | all-reduce | flops 2 | bytes 16 | tf_op jit(solution)/shard_map/psum | solution.py:28
  71.2 11.0 %all-reduce.8 = (f32[]{:T(128)}, f32[]{:T(128)}) all-reduce(f32[]{:T(128)} %get-tuple-element.24, f32[]{:T(128)} %get-tuple-element.25), channel_id=1, replica_groups=mesh['pb_0'=2,'pb_1'=8,'pb_2'=2,'dev_0'=4,'dev_1'=4] {'dev_0'}, use_global_device_ids=true, to_apply=%region_5.6 | all-reduce | flops 2 | bytes 16 | tf_op jit(solution)/shard_map/psum | solution.py:28
  82.2 9.0 %all-reduce.5 = (f32[]{:T(128)}, f32[]{:T(128)}) all-reduce(f32[]{:T(128)} %get-tuple-element.18, f32[]{:T(128)} %get-tuple-element.19), channel_id=1, replica_groups=mesh['pb_0'=2,'pb_1'=8,'pb_2'=2,'dev_0'=4,'dev_1'=4] {'dev_1'}, use_global_device_ids=true, to_apply=%region_6.7 | all-reduce | flops 2 | bytes 16 | tf_op jit(solution)/shard_map/psum | solution.py:28
  91.9 0.8 broadcast_in_dim.6
  92.8 5.4 %all-to-all-start.1 = ((f32[16,64,128]{2,1,0:T(8,128)}), f32[16,64,128]{2,1,0:T(8,128)S(1)}, u32[]{:S(2)}, u32[]{:S(2)}) async-start(f32[16,64,128]{2,1,0:T(8,128)} %broadcast_in_dim.6), calls=%async_computation.1 | async-start | bytes 1048576 | tf_op jit(solution)/shard_map/all_to_all | solution.py:34
  99.5 1.9 collective-permute-start
  102.1 11.2 %collective-permute-done = f32[256,128]{1,0:T(8,128)S(1)} collective-permute-done((f32[256,128]{1,0:T(8,128)S(1)}, f32[256,128]{1,0:T(8,128)S(1)}, u32[]{:S(2)}, u32[]{:S(2)}) %collective-permute-start) | collective-permute-done | bytes 131104 | tf_op jit(solution)/shard_map/ppermute | solution.py:50
  113.3 1.3 fusion.1
  114.6 1.8 fusion.27
  116.3 6.9 %all-to-all-start.2 = ((f32[16,64,128]{2,1,0:T(8,128)}), f32[16,64,128]{2,1,0:T(8,128)S(1)}, u32[]{:S(2)}, u32[]{:S(2)}) async-start(f32[16,64,128]{2,1,0:T(8,128)} %bitcast.6), calls=%async_computation.2 | async-start | bytes 1048576 | tf_op jit(solution)/shard_map/all_to_all | solution.py:22
  123.3 2.4 multiply_reduce_fusion.1
  125.7 7.3 %all-to-all-done.2 = f32[16,64,128]{2,1,0:T(8,128)S(1)} async-done(((f32[16,64,128]{2,1,0:T(8,128)}), f32[16,64,128]{2,1,0:T(8,128)S(1)}, u32[]{:S(2)}, u32[]{:S(2)}) %all-to-all-start.2) | async-done | bytes 524320 | tf_op jit(solution)/shard_map/all_to_all | solution.py:22
  133.0 0.6 multiply_reduce_fusion.4
  133.6 9.5 %all-reduce.13 = (f32[]{:T(128)}, f32[]{:T(128)}) all-reduce(f32[]{:T(128)} %multiply_reduce_fusion.4, f32[]{:T(128)} %get-tuple-element.40), channel_id=1, replica_groups=mesh['pb_0'=2,'pb_1'=8,'pb_2'=2,'dev_0'=4,'dev_1'=4] {'pb_0'}, use_global_device_ids=true, to_apply=%region_15.16 | all-reduce | flops 2 | bytes 16 | tf_op jit(solution)/shard_map/psum | solution.py:28
  143.1 14.8 %all-reduce.1 = (f32[]{:T(128)}, f32[]{:T(128)}) all-reduce(f32[]{:T(128)} %get-tuple-element.28, f32[]{:T(128)} %get-tuple-element.29), channel_id=1, replica_groups=mesh['pb_0'=2,'pb_1'=8,'pb_2'=2,'dev_0'=4,'dev_1'=4] {'pb_1'}, use_global_device_ids=true, to_apply=%region_16.17 | all-reduce | flops 2 | bytes 16 | tf_op jit(solution)/shard_map/psum | solution.py:28
  157.9 3.1 %all-reduce.10 = (f32[]{:T(128)}, f32[]{:T(128)}) all-reduce(f32[]{:T(128)} %get-tuple-element.4, f32[]{:T(128)} %get-tuple-element.5), channel_id=1, replica_groups=mesh['pb_0'=2,'pb_1'=8,'pb_2'=2,'dev_0'=4,'dev_1'=4] {'pb_2'}, use_global_device_ids=true, to_apply=%region_17.18 | all-reduce | flops 2 | bytes 16 | tf_op jit(solution)/shard_map/psum | solution.py:28
  161.0 11.0 %all-reduce.7 = (f32[]{:T(128)}, f32[]{:T(128)}) all-reduce(f32[]{:T(128)} %get-tuple-element.22, f32[]{:T(128)} %get-tuple-element.23), channel_id=1, replica_groups=mesh['pb_0'=2,'pb_1'=8,'pb_2'=2,'dev_0'=4,'dev_1'=4] {'dev_0'}, use_global_device_ids=true, to_apply=%region_18.19 | all-reduce | flops 2 | bytes 16 | tf_op jit(solution)/shard_map/psum | solution.py:28
  172.0 9.1 %all-reduce.4 = (f32[]{:T(128)}, f32[]{:T(128)}) all-reduce(f32[]{:T(128)} %get-tuple-element.16, f32[]{:T(128)} %get-tuple-element.17), channel_id=1, replica_groups=mesh['pb_0'=2,'pb_1'=8,'pb_2'=2,'dev_0'=4,'dev_1'=4] {'dev_1'}, use_global_device_ids=true, to_apply=%region_19.20 | all-reduce | flops 2 | bytes 16 | tf_op jit(solution)/shard_map/psum | solution.py:28
  181.9 0.8 broadcast_in_dim.7
  182.7 5.4 %all-to-all-start.3 = ((f32[16,64,128]{2,1,0:T(8,128)}), f32[16,64,128]{2,1,0:T(8,128)S(1)}, u32[]{:S(2)}, u32[]{:S(2)}) async-start(f32[16,64,128]{2,1,0:T(8,128)} %broadcast_in_dim.7), calls=%async_computation.3 | async-start | bytes 1048576 | tf_op jit(solution)/shard_map/all_to_all | solution.py:34
  189.3 2.1 collective-permute-start.1
  192.2 10.9 %collective-permute-done.1 = f32[256,128]{1,0:T(8,128)S(1)} collective-permute-done((f32[256,128]{1,0:T(8,128)S(1)}, f32[256,128]{1,0:T(8,128)S(1)}, u32[]{:S(2)}, u32[]{:S(2)}) %collective-permute-start.1) | collective-permute-done | bytes 131104 | tf_op jit(solution)/shard_map/ppermute | solution.py:50
  203.1 1.3 fusion
  204.4 1.8 fusion.28
  206.1 6.5 %all-to-all-start.4 = ((f32[16,64,128]{2,1,0:T(8,128)}), f32[16,64,128]{2,1,0:T(8,128)S(1)}, u32[]{:S(2)}, u32[]{:S(2)}) async-start(f32[16,64,128]{2,1,0:T(8,128)} %bitcast.10), calls=%async_computation.4 | async-start | bytes 1048576 | tf_op jit(solution)/shard_map/all_to_all | solution.py:22
  212.7 2.5 multiply_reduce_fusion
  215.2 7.2 %all-to-all-done.4 = f32[16,64,128]{2,1,0:T(8,128)S(1)} async-done(((f32[16,64,128]{2,1,0:T(8,128)}), f32[16,64,128]{2,1,0:T(8,128)S(1)}, u32[]{:S(2)}, u32[]{:S(2)}) %all-to-all-start.4) | async-done | bytes 524320 | tf_op jit(solution)/shard_map/all_to_all | solution.py:22
  223.1 9.5 %all-reduce.12 = (f32[]{:T(128)}, f32[]{:T(128)}) all-reduce(f32[]{:T(128)} %multiply_reduce_fusion.3, f32[]{:T(128)} %get-tuple-element.42), channel_id=1, replica_groups=mesh['pb_0'=2,'pb_1'=8,'pb_2'=2,'dev_0'=4,'dev_1'=4] {'pb_0'}, use_global_device_ids=true, to_apply=%region_28.29 | all-reduce | flops 2 | bytes 16 | tf_op jit(solution)/shard_map/psum | solution.py:28
  232.5 16.5 %all-reduce = (f32[]{:T(128)}, f32[]{:T(128)}) all-reduce(f32[]{:T(128)} %get-tuple-element.26, f32[]{:T(128)} %get-tuple-element.27), channel_id=1, replica_groups=mesh['pb_0'=2,'pb_1'=8,'pb_2'=2,'dev_0'=4,'dev_1'=4] {'pb_1'}, use_global_device_ids=true, to_apply=%region_29.30 | all-reduce | flops 2 | bytes 16 | tf_op jit(solution)/shard_map/psum | solution.py:28
  249.0 3.1 %all-reduce.9 = (f32[]{:T(128)}, f32[]{:T(128)}) all-reduce(f32[]{:T(128)} %get-tuple-element.2, f32[]{:T(128)} %get-tuple-element.3), channel_id=1, replica_groups=mesh['pb_0'=2,'pb_1'=8,'pb_2'=2,'dev_0'=4,'dev_1'=4] {'pb_2'}, use_global_device_ids=true, to_apply=%region_30.31 | all-reduce | flops 2 | bytes 16 | tf_op jit(solution)/shard_map/psum | solution.py:28
  252.1 11.2 %all-reduce.6 = (f32[]{:T(128)}, f32[]{:T(128)}) all-reduce(f32[]{:T(128)} %get-tuple-element.20, f32[]{:T(128)} %get-tuple-element.21), channel_id=1, replica_groups=mesh['pb_0'=2,'pb_1'=8,'pb_2'=2,'dev_0'=4,'dev_1'=4] {'dev_0'}, use_global_device_ids=true, to_apply=%region_31.32 | all-reduce | flops 2 | bytes 16 | tf_op jit(solution)/shard_map/psum | solution.py:28
  263.2 9.5 %all-reduce.3 = (f32[]{:T(128)}, f32[]{:T(128)}) all-reduce(f32[]{:T(128)} %get-tuple-element.14, f32[]{:T(128)} %get-tuple-element.15), channel_id=1, replica_groups=mesh['pb_0'=2,'pb_1'=8,'pb_2'=2,'dev_0'=4,'dev_1'=4] {'dev_1'}, use_global_device_ids=true, to_apply=%region_32.33 | all-reduce | flops 2 | bytes 16 | tf_op jit(solution)/shard_map/psum | solution.py:28
  273.4 0.8 broadcast_in_dim.16
  274.3 5.8 %all-to-all-start.5 = ((f32[16,64,128]{2,1,0:T(8,128)}), f32[16,64,128]{2,1,0:T(8,128)S(1)}, u32[]{:S(2)}, u32[]{:S(2)}) async-start(f32[16,64,128]{2,1,0:T(8,128)} %broadcast_in_dim.16), calls=%async_computation.5 | async-start | bytes 1048576 | tf_op jit(solution)/shard_map/all_to_all | solution.py:34
  280.8 1.9 collective-permute-start.2
  282.8 11.8 %collective-permute-done.2 = f32[256,128]{1,0:T(8,128)S(1)} collective-permute-done((f32[256,128]{1,0:T(8,128)S(1)}, f32[256,128]{1,0:T(8,128)S(1)}, u32[]{:S(2)}, u32[]{:S(2)}) %collective-permute-start.2) | collective-permute-done | bytes 131104 | tf_op jit(solution)/shard_map/ppermute | solution.py:50
  294.5 0.8 copy.9
  295.3 0.7 copy.10
  (25 shorter events, 0.9 us)
Async XLA Ops:
  0.6 10.1 %copy-start.1 = (f32[256,128]{1,0:T(8,128)S(1)}, f32[256,128]{1,0:T(8,128)}, u32[]{:S(2)}) copy-start(f32[256,128]{1,0:T(8,128)} %param.6) | copy-start | bytes 393220
  10.0 0.7 copy-start.2
  14.9 10.4 %copy-start = (f32[1024,128]{1,0:T(8,128)S(1)}, f32[1024,128]{1,0:T(8,128)}, u32[]{:S(2)}) copy-start(f32[1024,128]{1,0:T(8,128)} %param.5) | copy-start | bytes 1572868
  14.9 24.3 %all-to-all-start = ((f32[16,64,128]{2,1,0:T(8,128)}), f32[16,64,128]{2,1,0:T(8,128)S(1)}, u32[]{:S(2)}, u32[]{:S(2)}) async-start(f32[16,64,128]{2,1,0:T(8,128)} %bitcast.2), calls=%async_computation | async-start | bytes 1048576 | tf_op jit(solution)/shard_map/all_to_all | solution.py:22
  92.8 20.5 %all-to-all-start.1 = ((f32[16,64,128]{2,1,0:T(8,128)}), f32[16,64,128]{2,1,0:T(8,128)S(1)}, u32[]{:S(2)}, u32[]{:S(2)}) async-start(f32[16,64,128]{2,1,0:T(8,128)} %broadcast_in_dim.6), calls=%async_computation.1 | async-start | bytes 1048576 | tf_op jit(solution)/shard_map/all_to_all | solution.py:34
  99.5 13.7 %collective-permute-start = (f32[256,128]{1,0:T(8,128)S(1)}, f32[256,128]{1,0:T(8,128)S(1)}, u32[]{:S(2)}, u32[]{:S(2)}) collective-permute-start(f32[256,128]{1,0:T(8,128)S(1)} %multiply_add_fusion.2), channel_id=1, source_target_pairs={{0,16},{16,32},{32,48},{48,64},{64,80},{80,96},{96,112},{112,128},... | collective-permute-start | bytes 393224 | tf_op jit(solution)/shard_map/ppermute | solution.py:50
  116.3 16.7 %all-to-all-start.2 = ((f32[16,64,128]{2,1,0:T(8,128)}), f32[16,64,128]{2,1,0:T(8,128)S(1)}, u32[]{:S(2)}, u32[]{:S(2)}) async-start(f32[16,64,128]{2,1,0:T(8,128)} %bitcast.6), calls=%async_computation.2 | async-start | bytes 1048576 | tf_op jit(solution)/shard_map/all_to_all | solution.py:22
  182.7 20.4 %all-to-all-start.3 = ((f32[16,64,128]{2,1,0:T(8,128)}), f32[16,64,128]{2,1,0:T(8,128)S(1)}, u32[]{:S(2)}, u32[]{:S(2)}) async-start(f32[16,64,128]{2,1,0:T(8,128)} %broadcast_in_dim.7), calls=%async_computation.3 | async-start | bytes 1048576 | tf_op jit(solution)/shard_map/all_to_all | solution.py:34
  189.3 13.7 %collective-permute-start.1 = (f32[256,128]{1,0:T(8,128)S(1)}, f32[256,128]{1,0:T(8,128)S(1)}, u32[]{:S(2)}, u32[]{:S(2)}) collective-permute-start(f32[256,128]{1,0:T(8,128)S(1)} %multiply_add_fusion.1), channel_id=1, source_target_pairs={{0,16},{16,32},{32,48},{48,64},{64,80},{80,96},{96,112},{112,128},... | collective-permute-start | bytes 393224 | tf_op jit(solution)/shard_map/ppermute | solution.py:50
  206.1 16.3 %all-to-all-start.4 = ((f32[16,64,128]{2,1,0:T(8,128)}), f32[16,64,128]{2,1,0:T(8,128)S(1)}, u32[]{:S(2)}, u32[]{:S(2)}) async-start(f32[16,64,128]{2,1,0:T(8,128)} %bitcast.10), calls=%async_computation.4 | async-start | bytes 1048576 | tf_op jit(solution)/shard_map/all_to_all | solution.py:22
  274.3 20.3 %all-to-all-start.5 = ((f32[16,64,128]{2,1,0:T(8,128)}), f32[16,64,128]{2,1,0:T(8,128)S(1)}, u32[]{:S(2)}, u32[]{:S(2)}) async-start(f32[16,64,128]{2,1,0:T(8,128)} %broadcast_in_dim.16), calls=%async_computation.5 | async-start | bytes 1048576 | tf_op jit(solution)/shard_map/all_to_all | solution.py:34
  280.8 13.7 %collective-permute-start.2 = (f32[256,128]{1,0:T(8,128)S(1)}, f32[256,128]{1,0:T(8,128)S(1)}, u32[]{:S(2)}, u32[]{:S(2)}) collective-permute-start(f32[256,128]{1,0:T(8,128)S(1)} %multiply_add_fusion), channel_id=1, source_target_pairs={{0,16},{16,32},{32,48},{48,64},{64,80},{80,96},{96,112},{112,128},... | collective-permute-start | bytes 393224 | tf_op jit(solution)/shard_map/ppermute | solution.py:50
where the time goes:
time: 297 us; the launch traced here: 296 us
  blocking collectives  149 us (50%)
  waiting for transfers between devices  59.9 us (20%)
  starting transfers between devices  46.4 us (16%)
  matrix products  17.6 us (6%)
  between operations  14.6 us (5%)
  local copies, waits for them, and re-layouts  6.86 us (2%)
    psum x15, blocking collectives, one_axis_at_a_time(): array = lax.psum(array, axis)  149 us
    ppermute x3, waiting for transfers between devices, shifted(): lax.ppermute(array, axis, [(i, (i + by) % size) for i in range(size)])  33.9 us
    all_to_all x3, waiting for transfers between devices, sent_and_summed(): parts = lax.all_to_all(in_blocks(array, dim, size), axis, 0, 0, tiled=True)  26 us
    all_to_all x3, starting transfers between devices, sent_and_summed(): parts = lax.all_to_all(in_blocks(array, dim, size), axis, 0, 0, tiled=True)  23.9 us
    all_to_all x3, starting transfers between devices, sent_to_all(): return lax.all_to_all(copies, axis, split_axis=0, concat_axis=0, tiled=True)  16.6 us
    dot_general x3, matrix products, per_device(): grad_v = jnp.dot(weighted.T, factors, precision=lax.Precision.HIGHEST)  7.35 us
    ppermute x3, starting transfers between devices, shifted(): lax.ppermute(array, axis, [(i, (i + by) % size) for i in range(size)])  5.94 us
  transfers between devices with their start and end apart: 9, of which 6 were waited for; matrix products, arithmetic and copies ran while one was open for 3% of the time, Pallas kernels for 0%

commit v1 on v0

--- a/solution.py
+++ b/solution.py
@@ -25,7 +25,7 @@
 
 def one_axis_at_a_time(array, axes):
     for axis in axes:
-        array = lax.psum(array, axis)
+        array = jnp.sum(lax.all_gather(array, axis), axis=0)
     return array
 
 

time: 297 us -> 347 us (1.17)
  local copies, waits for them, and re-layouts: 6.86 us -> 54 us
  other arithmetic: 2.06 us -> 20.2 us
  blocking collectives: 149 us -> 137 us
  waiting for transfers between devices: 59.9 us -> 54.9 us
    psum x15 -> x0, blocking collectives: 149 us -> none  [one_axis_at_a_time(): array = lax.psum(array, axis)]
    unnamed x0 -> x15, blocking collectives: none -> 137 us
    unnamed x8 -> x73, local copies, waits for them, and re-layouts: 1.46 us -> 48.6 us
    reduce_sum x0 -> x30, other arithmetic: none -> 18.2 us  [one_axis_at_a_time(): array = jnp.sum(lax.all_gather(array, axis), axis=0)]
    all_to_all x3, waiting for transfers between devices: 26 us -> 20.9 us  [sent_and_summed(): parts = lax.all_to_all(in_blocks(array, dim, size), axis, 0, 0, tiled=True)]
  transfers between devices with their start and end apart: 9 -> 9, of which waited for: 6 -> 6; matrix products, arithmetic and copies ran while one was open for 3% -> 4% of each run, Pallas kernels for 0% -> 0%
where the time goes in v1:
time: 347 us; the launch traced here: 345 us
  blocking collectives  137 us (39%)
  waiting for transfers between devices  54.9 us (16%)
  local copies, waits for them, and re-layouts  54 us (16%)
  starting transfers between devices  46.2 us (13%)
  other arithmetic  20.2 us (6%)
  matrix products  17.6 us (5%)
  between operations  14.7 us (4%)
    unnamed x15, blocking collectives  137 us
    unnamed x73, local copies, waits for them, and re-layouts  48.6 us
    ppermute x3, waiting for transfers between devices, shifted(): lax.ppermute(array, axis, [(i, (i + by) % size) for i in range(size)])  34 us
    all_to_all x3, starting transfers between devices, sent_and_summed(): parts = lax.all_to_all(in_blocks(array, dim, size), axis, 0, 0, tiled=True)  24 us
    all_to_all x3, waiting for transfers between devices, sent_and_summed(): parts = lax.all_to_all(in_blocks(array, dim, size), axis, 0, 0, tiled=True)  20.9 us
    reduce_sum x30, other arithmetic, one_axis_at_a_time(): array = jnp.sum(lax.all_gather(array, axis), axis=0)  18.2 us
    all_to_all x3, starting transfers between devices, sent_to_all(): return lax.all_to_all(copies, axis, split_axis=0, concat_axis=0, tiled=True)  16.5 us
    dot_general x3, matrix products, per_device(): grad_v = jnp.dot(weighted.T, factors, precision=lax.Precision.HIGHEST)  7.3 us
  transfers between devices with their start and end apart: 9, of which 6 were waited for; matrix products, arithmetic and copies ran while one was open for 4% of the time, Pallas kernels for 0%

profile of v1, /device:TPU:2, one launch (start us, length us, event | category | flops | bytes accessed | tf_op | source)
XLA Modules:
  0.0 345.1 jit_solution(6258377669720477899)
XLA Ops:
  8.5 1.5 fusion.24
  10.7 2.3 fusion.2
  13.0 1.8 fusion.26
  14.8 10.4 %all-to-all-start = ((f32[16,64,128]{2,1,0:T(8,128)}), f32[16,64,128]{2,1,0:T(8,128)S(1)}, u32[]{:S(2)}, u32[]{:S(2)}) async-start(f32[16,64,128]{2,1,0:T(8,128)} %bitcast.2), calls=%async_computation | async-start | bytes 1048576 | tf_op jit(solution)/shard_map/all_to_all | solution.py:22
  26.5 2.4 multiply_reduce_fusion.2
  30.2 8.9 %all-to-all-done = f32[16,64,128]{2,1,0:T(8,128)S(1)} async-done(((f32[16,64,128]{2,1,0:T(8,128)}), f32[16,64,128]{2,1,0:T(8,128)S(1)}, u32[]{:S(2)}, u32[]{:S(2)}) %all-to-all-start) | async-done | bytes 524320 | tf_op jit(solution)/shard_map/all_to_all | solution.py:22
  42.4 9.2 %all-reduce.44 = (f32[2]{0:T(128)S(1)}, f32[2]{0:T(128)S(1)}) all-reduce(f32[2]{0:T(128)S(1)} %dynamic-update-slice, f32[2]{0:T(128)S(1)} %dynamic-update-slice.5), channel_id=1, replica_groups=mesh['pb_0'=2,'pb_1'=8,'pb_2'=2,'dev_0'=4,'dev_1'=4] {'pb_0'}, use_global_device_ids=true, to_apply=%add | all-reduce | flops 4 | bytes 32
  54.2 1.4 dynamic-update-slice.1
  56.8 17.6 %all-reduce.32 = (f32[8]{0:T(128)S(1)}, f32[8]{0:T(128)S(1)}) all-reduce(f32[8]{0:T(128)S(1)} %dynamic-update-slice.1, f32[8]{0:T(128)S(1)} %dynamic-update-slice.6), channel_id=1, replica_groups=mesh['pb_0'=2,'pb_1'=8,'pb_2'=2,'dev_0'=4,'dev_1'=4] {'pb_1'}, use_global_device_ids=true, to_apply=%add.1 | all-reduce | flops 16 | bytes 128
  79.5 2.4 all-reduce.41
  87.3 10.4 %all-reduce.38 = (f32[4]{0:T(128)S(1)}, f32[4]{0:T(128)S(1)}) all-reduce(f32[4]{0:T(128)S(1)} %dynamic-update-slice.3, f32[4]{0:T(128)S(1)} %dynamic-update-slice.8), channel_id=1, replica_groups=mesh['pb_0'=2,'pb_1'=8,'pb_2'=2,'dev_0'=4,'dev_1'=4] {'dev_0'}, use_global_device_ids=true, to_apply=%add.3 | all-reduce | flops 8 | bytes 64
  100.2 1.4 dynamic-update-slice.4
  101.7 8.3 %all-reduce.35 = (f32[4]{0:T(128)S(1)}, f32[4]{0:T(128)S(1)}) all-reduce(f32[4]{0:T(128)S(1)} %dynamic-update-slice.4, f32[4]{0:T(128)S(1)} %dynamic-update-slice.9), channel_id=1, replica_groups=mesh['pb_0'=2,'pb_1'=8,'pb_2'=2,'dev_0'=4,'dev_1'=4] {'dev_1'}, use_global_device_ids=true, to_apply=%add.4 | all-reduce | flops 8 | bytes 64
  112.2 5.4 %all-to-all-start.1 = ((f32[16,64,128]{2,1,0:T(8,128)}), f32[16,64,128]{2,1,0:T(8,128)S(1)}, u32[]{:S(2)}, u32[]{:S(2)}) async-start(f32[16,64,128]{2,1,0:T(8,128)} %broadcast_in_dim.6), calls=%async_computation.1 | async-start | bytes 1048576 | tf_op jit(solution)/shard_map/all_to_all | solution.py:34
  119.5 1.9 collective-permute-start
  122.1 11.1 %collective-permute-done = f32[256,128]{1,0:T(8,128)S(1)} collective-permute-done((f32[256,128]{1,0:T(8,128)S(1)}, f32[256,128]{1,0:T(8,128)S(1)}, u32[]{:S(2)}, u32[]{:S(2)}) %collective-permute-start) | collective-permute-done | bytes 131104 | tf_op jit(solution)/shard_map/ppermute | solution.py:50
  134.5 1.8 fusion.27
  136.3 6.9 %all-to-all-start.2 = ((f32[16,64,128]{2,1,0:T(8,128)}), f32[16,64,128]{2,1,0:T(8,128)S(1)}, u32[]{:S(2)}, u32[]{:S(2)}) async-start(f32[16,64,128]{2,1,0:T(8,128)} %bitcast.21), calls=%async_computation.2 | async-start | bytes 1048576 | tf_op jit(solution)/shard_map/all_to_all | solution.py:22
  143.2 2.5 multiply_reduce_fusion.1
  147.0 6.0 %all-to-all-done.2 = f32[16,64,128]{2,1,0:T(8,128)S(1)} async-done(((f32[16,64,128]{2,1,0:T(8,128)}), f32[16,64,128]{2,1,0:T(8,128)S(1)}, u32[]{:S(2)}, u32[]{:S(2)}) %all-to-all-start.2) | async-done | bytes 524320 | tf_op jit(solution)/shard_map/all_to_all | solution.py:22
  154.9 8.8 %all-reduce.43 = (f32[2]{0:T(128)S(1)}, f32[2]{0:T(128)S(1)}) all-reduce(f32[2]{0:T(128)S(1)} %dynamic-update-slice.10, f32[2]{0:T(128)S(1)} %dynamic-update-slice.15), channel_id=1, replica_groups=mesh['pb_0'=2,'pb_1'=8,'pb_2'=2,'dev_0'=4,'dev_1'=4] {'pb_0'}, use_global_device_ids=true, to_apply=%add.10 | all-reduce | flops 4 | bytes 32
  164.3 1.4 dynamic-update-slice.16
  166.3 1.4 dynamic-update-slice.11
  167.7 14.1 %all-reduce.31 = (f32[8]{0:T(128)S(1)}, f32[8]{0:T(128)S(1)}) all-reduce(f32[8]{0:T(128)S(1)} %dynamic-update-slice.11, f32[8]{0:T(128)S(1)} %dynamic-update-slice.16), channel_id=1, replica_groups=mesh['pb_0'=2,'pb_1'=8,'pb_2'=2,'dev_0'=4,'dev_1'=4] {'pb_1'}, use_global_device_ids=true, to_apply=%add.11 | all-reduce | flops 16 | bytes 128
  185.8 2.4 all-reduce.40
  192.1 10.4 %all-reduce.37 = (f32[4]{0:T(128)S(1)}, f32[4]{0:T(128)S(1)}) all-reduce(f32[4]{0:T(128)S(1)} %dynamic-update-slice.13, f32[4]{0:T(128)S(1)} %dynamic-update-slice.18), channel_id=1, replica_groups=mesh['pb_0'=2,'pb_1'=8,'pb_2'=2,'dev_0'=4,'dev_1'=4] {'dev_0'}, use_global_device_ids=true, to_apply=%add.13 | all-reduce | flops 8 | bytes 64
  203.0 1.4 dynamic-update-slice.19
  205.1 1.4 dynamic-update-slice.14
  206.5 8.5 %all-reduce.34 = (f32[4]{0:T(128)S(1)}, f32[4]{0:T(128)S(1)}) all-reduce(f32[4]{0:T(128)S(1)} %dynamic-update-slice.14, f32[4]{0:T(128)S(1)} %dynamic-update-slice.19), channel_id=1, replica_groups=mesh['pb_0'=2,'pb_1'=8,'pb_2'=2,'dev_0'=4,'dev_1'=4] {'dev_1'}, use_global_device_ids=true, to_apply=%add.14 | all-reduce | flops 8 | bytes 64
  217.2 5.3 %all-to-all-start.3 = ((f32[16,64,128]{2,1,0:T(8,128)}), f32[16,64,128]{2,1,0:T(8,128)S(1)}, u32[]{:S(2)}, u32[]{:S(2)}) async-start(f32[16,64,128]{2,1,0:T(8,128)} %broadcast_in_dim.7), calls=%async_computation.3 | async-start | bytes 1048576 | tf_op jit(solution)/shard_map/all_to_all | solution.py:34
  224.5 1.9 collective-permute-start.1
  227.1 11.1 %collective-permute-done.1 = f32[256,128]{1,0:T(8,128)S(1)} collective-permute-done((f32[256,128]{1,0:T(8,128)S(1)}, f32[256,128]{1,0:T(8,128)S(1)}, u32[]{:S(2)}, u32[]{:S(2)}) %collective-permute-start.1) | collective-permute-done | bytes 131104 | tf_op jit(solution)/shard_map/ppermute | solution.py:50
  239.5 1.8 fusion.28
  241.2 6.6 %all-to-all-start.4 = ((f32[16,64,128]{2,1,0:T(8,128)}), f32[16,64,128]{2,1,0:T(8,128)S(1)}, u32[]{:S(2)}, u32[]{:S(2)}) async-start(f32[16,64,128]{2,1,0:T(8,128)} %bitcast.35), calls=%async_computation.4 | async-start | bytes 1048576 | tf_op jit(solution)/shard_map/all_to_all | solution.py:22
  247.9 2.4 multiply_reduce_fusion
  251.6 6.0 %all-to-all-done.4 = f32[16,64,128]{2,1,0:T(8,128)S(1)} async-done(((f32[16,64,128]{2,1,0:T(8,128)}), f32[16,64,128]{2,1,0:T(8,128)S(1)}, u32[]{:S(2)}, u32[]{:S(2)}) %all-to-all-start.4) | async-done | bytes 524320 | tf_op jit(solution)/shard_map/all_to_all | solution.py:22
  259.6 8.8 %all-reduce.42 = (f32[2]{0:T(128)S(1)}, f32[2]{0:T(128)S(1)}) all-reduce(f32[2]{0:T(128)S(1)} %dynamic-update-slice.20, f32[2]{0:T(128)S(1)} %dynamic-update-slice.25), channel_id=1, replica_groups=mesh['pb_0'=2,'pb_1'=8,'pb_2'=2,'dev_0'=4,'dev_1'=4] {'pb_0'}, use_global_device_ids=true, to_apply=%add.20 | all-reduce | flops 4 | bytes 32
  269.0 1.4 dynamic-update-slice.26
  271.0 1.4 dynamic-update-slice.21
  272.4 14.9 %all-reduce.30 = (f32[8]{0:T(128)S(1)}, f32[8]{0:T(128)S(1)}) all-reduce(f32[8]{0:T(128)S(1)} %dynamic-update-slice.21, f32[8]{0:T(128)S(1)} %dynamic-update-slice.26), channel_id=1, replica_groups=mesh['pb_0'=2,'pb_1'=8,'pb_2'=2,'dev_0'=4,'dev_1'=4] {'pb_1'}, use_global_device_ids=true, to_apply=%add.21 | all-reduce | flops 16 | bytes 128
  291.3 2.4 all-reduce.39
  297.5 10.4 %all-reduce.36 = (f32[4]{0:T(128)S(1)}, f32[4]{0:T(128)S(1)}) all-reduce(f32[4]{0:T(128)S(1)} %dynamic-update-slice.23, f32[4]{0:T(128)S(1)} %dynamic-update-slice.28), channel_id=1, replica_groups=mesh['pb_0'=2,'pb_1'=8,'pb_2'=2,'dev_0'=4,'dev_1'=4] {'dev_0'}, use_global_device_ids=true, to_apply=%add.23 | all-reduce | flops 8 | bytes 64
  308.6 1.4 dynamic-update-slice.29
  310.6 1.4 dynamic-update-slice.24
  312.1 8.6 %all-reduce.33 = (f32[4]{0:T(128)S(1)}, f32[4]{0:T(128)S(1)}) all-reduce(f32[4]{0:T(128)S(1)} %dynamic-update-slice.24, f32[4]{0:T(128)S(1)} %dynamic-update-slice.29), channel_id=1, replica_groups=mesh['pb_0'=2,'pb_1'=8,'pb_2'=2,'dev_0'=4,'dev_1'=4] {'dev_1'}, use_global_device_ids=true, to_apply=%add.24 | all-reduce | flops 8 | bytes 64
  322.9 5.8 %all-to-all-start.5 = ((f32[16,64,128]{2,1,0:T(8,128)}), f32[16,64,128]{2,1,0:T(8,128)S(1)}, u32[]{:S(2)}, u32[]{:S(2)}) async-start(f32[16,64,128]{2,1,0:T(8,128)} %broadcast_in_dim.16), calls=%async_computation.5 | async-start | bytes 1048576 | tf_op jit(solution)/shard_map/all_to_all | solution.py:34
  330.0 1.9 collective-permute-start.2
  331.9 11.8 %collective-permute-done.2 = f32[256,128]{1,0:T(8,128)S(1)} collective-permute-done((f32[256,128]{1,0:T(8,128)S(1)}, f32[256,128]{1,0:T(8,128)S(1)}, u32[]{:S(2)}, u32[]{:S(2)}) %collective-permute-start.2) | collective-permute-done | bytes 131104 | tf_op jit(solution)/shard_map/ppermute | solution.py:50
  (120 shorter events, 61.2 us)
Async XLA Ops:
  0.6 10.0 %copy-start.1 = (f32[256,128]{1,0:T(8,128)S(1)}, f32[256,128]{1,0:T(8,128)}, u32[]{:S(2)}) copy-start(f32[256,128]{1,0:T(8,128)} %param.6) | copy-start | bytes 393220
  10.0 0.7 copy-start.2
  14.8 11.7 %copy-start = (f32[1024,128]{1,0:T(8,128)S(1)}, f32[1024,128]{1,0:T(8,128)}, u32[]{:S(2)}) copy-start(f32[1024,128]{1,0:T(8,128)} %param.5) | copy-start | bytes 1572868
  14.8 24.3 %all-to-all-start = ((f32[16,64,128]{2,1,0:T(8,128)}), f32[16,64,128]{2,1,0:T(8,128)S(1)}, u32[]{:S(2)}, u32[]{:S(2)}) async-start(f32[16,64,128]{2,1,0:T(8,128)} %bitcast.2), calls=%async_computation | async-start | bytes 1048576 | tf_op jit(solution)/shard_map/all_to_all | solution.py:22
  112.2 21.1 %all-to-all-start.1 = ((f32[16,64,128]{2,1,0:T(8,128)}), f32[16,64,128]{2,1,0:T(8,128)S(1)}, u32[]{:S(2)}, u32[]{:S(2)}) async-start(f32[16,64,128]{2,1,0:T(8,128)} %broadcast_in_dim.6), calls=%async_computation.1 | async-start | bytes 1048576 | tf_op jit(solution)/shard_map/all_to_all | solution.py:34
  119.5 13.7 %collective-permute-start = (f32[256,128]{1,0:T(8,128)S(1)}, f32[256,128]{1,0:T(8,128)S(1)}, u32[]{:S(2)}, u32[]{:S(2)}) collective-permute-start(f32[256,128]{1,0:T(8,128)S(1)} %multiply_add_fusion.2), channel_id=1, source_target_pairs={{0,16},{16,32},{32,48},{48,64},{64,80},{80,96},{96,112},{112,128},... | collective-permute-start | bytes 393224 | tf_op jit(solution)/shard_map/ppermute | solution.py:50
  136.3 16.6 %all-to-all-start.2 = ((f32[16,64,128]{2,1,0:T(8,128)}), f32[16,64,128]{2,1,0:T(8,128)S(1)}, u32[]{:S(2)}, u32[]{:S(2)}) async-start(f32[16,64,128]{2,1,0:T(8,128)} %bitcast.21), calls=%async_computation.2 | async-start | bytes 1048576 | tf_op jit(solution)/shard_map/all_to_all | solution.py:22
  217.2 21.0 %all-to-all-start.3 = ((f32[16,64,128]{2,1,0:T(8,128)}), f32[16,64,128]{2,1,0:T(8,128)S(1)}, u32[]{:S(2)}, u32[]{:S(2)}) async-start(f32[16,64,128]{2,1,0:T(8,128)} %broadcast_in_dim.7), calls=%async_computation.3 | async-start | bytes 1048576 | tf_op jit(solution)/shard_map/all_to_all | solution.py:34
  224.5 13.7 %collective-permute-start.1 = (f32[256,128]{1,0:T(8,128)S(1)}, f32[256,128]{1,0:T(8,128)S(1)}, u32[]{:S(2)}, u32[]{:S(2)}) collective-permute-start(f32[256,128]{1,0:T(8,128)S(1)} %multiply_add_fusion.1), channel_id=1, source_target_pairs={{0,16},{16,32},{32,48},{48,64},{64,80},{80,96},{96,112},{112,128},... | collective-permute-start | bytes 393224 | tf_op jit(solution)/shard_map/ppermute | solution.py:50
  241.2 16.4 %all-to-all-start.4 = ((f32[16,64,128]{2,1,0:T(8,128)}), f32[16,64,128]{2,1,0:T(8,128)S(1)}, u32[]{:S(2)}, u32[]{:S(2)}) async-start(f32[16,64,128]{2,1,0:T(8,128)} %bitcast.35), calls=%async_computation.4 | async-start | bytes 1048576 | tf_op jit(solution)/shard_map/all_to_all | solution.py:22
  322.9 20.8 %all-to-all-start.5 = ((f32[16,64,128]{2,1,0:T(8,128)}), f32[16,64,128]{2,1,0:T(8,128)S(1)}, u32[]{:S(2)}, u32[]{:S(2)}) async-start(f32[16,64,128]{2,1,0:T(8,128)} %broadcast_in_dim.16), calls=%async_computation.5 | async-start | bytes 1048576 | tf_op jit(solution)/shard_map/all_to_all | solution.py:34
  330.0 13.7 %collective-permute-start.2 = (f32[256,128]{1,0:T(8,128)S(1)}, f32[256,128]{1,0:T(8,128)S(1)}, u32[]{:S(2)}, u32[]{:S(2)}) collective-permute-start(f32[256,128]{1,0:T(8,128)S(1)} %multiply_add_fusion), channel_id=1, source_target_pairs={{0,16},{16,32},{32,48},{48,64},{64,80},{80,96},{96,112},{112,128},... | collective-permute-start | bytes 393224 | tf_op jit(solution)/shard_map/ppermute | solution.py:50
